TPU v7x, 256 devices: a whole 4x4x8 slice. The times are simulated.
256 devices in a mesh: ctx: 64 (over x_lo, z, y), fsdp: 4 (over x_hi, core).
Axes of the slice: x: 4 (x_hi: 2, x_lo: 2; x = x_hi * 2 + x_lo), y: 4, z: 8, core: 2. Of those that a mesh axis runs over, the one named last changes fastest.
Arguments:
- q_raw: bfloat16 [8192, 2560], P('ctx', 'fsdp'), may hold values from -3000 to 3000
- k_raw: bfloat16 [8192, 2560], P('ctx', 'fsdp'), may hold values from -3000 to 3000
- values: bfloat16 [8192, 2560], P('ctx', 'fsdp'), may hold values from -6 to 6
- positions: int32 [8192, 3], P('ctx'), may hold values from 0 to 79, as said below
- cotangent: bfloat16 [8192, 5120], P('ctx'), may hold values from -6 to 6
- out_weight: bfloat16 [2560, 5120], P('fsdp'), may hold values from -0.078125 to 0.078125
- modulation: float32 [50, 5120], replicated, may hold values from -4 to 4
- step_index: int32 [1], replicated, may hold values from 0 to 49
Outputs:
- query_grad: bfloat16 [8192, 2560], P('ctx', 'fsdp')
- key_grad: bfloat16 [8192, 2560], P('ctx', 'fsdp')
- value_grad: bfloat16 [8192, 2560], P('ctx', 'fsdp')
Inputs may be any that keep to these rules, and one draw needn't show every extreme that they name: `positions`: frame, row and column coordinates of each token in the latent grid.
All inputs are finite; a program needn't handle non-finite values.
Results may differ from a plain program's by a relative error of at most 0.034.
Values may be sent and summed in bfloat16 or wider, within the bound.
No kernel may reach another device: no remote copies, remote signals or barrier semaphores. Data moves between devices by JAX's collectives and lax.ppermute only.
A program may use at most 192 MiB of HBM per device.

v0:
```python
import math

import jax
import jax.numpy as jnp
import numpy as np
from jax import lax
from jax.sharding import PartitionSpec as P

HEAD_DIM = 128


EPSILON = 1e-06
NEG_LARGE = -1e30


def angle_table(head_size):
    side_dim = 2 * (head_size // 6)
    first_dim = head_size - 2 * side_dim
    freq_table = np.zeros((3, head_size // 2), np.float32)
    column = 0
    for axis_number, group_dim in enumerate([first_dim, side_dim, side_dim]):
        for pair_index in range(group_dim // 2):
            freq_table[axis_number, column] = 10000.0 ** (-2.0 * pair_index / group_dim)
            column += 1
    return freq_table


def rotation(positions, heads_count, head_size):
    angles = jnp.dot(
        positions.astype(jnp.float32),
        jnp.asarray(angle_table(head_size)),
        precision=lax.Precision.HIGHEST,
    )
    doubled = jnp.repeat(angles, 2, axis=1)
    cosine = jnp.tile(jnp.cos(doubled), (1, heads_count))
    sine_full = jnp.tile(jnp.sin(doubled), (1, heads_count))
    parity = jnp.tile(jnp.array([-1.0, 1.0], jnp.float32), heads_count * head_size // 2)
    return (cosine, sine_full * parity[None, :])


def rotate(source, cosine, signed_sine, direction):
    column_ids = jnp.arange(source.shape[1])
    partner = jnp.where(
        column_ids % 2 == 0, jnp.roll(source, -1, axis=1), jnp.roll(source, 1, axis=1)
    )
    return source * cosine + direction * partner * signed_sine


def split_heads(matrix):
    return matrix.reshape(matrix.shape[0], matrix.shape[1] // HEAD_DIM, HEAD_DIM)


def join_heads(tensor):
    return jnp.transpose(tensor, (1, 0, 2)).reshape(
        tensor.shape[1], tensor.shape[0] * tensor.shape[2]
    )


def shards(q_raw, k_raw, values, positions, cotangent, out_weight, modulation, step_index):
    tokens_here = q_raw.shape[0]
    width_here = q_raw.shape[1]
    heads_here = width_here // HEAD_DIM
    inner_width = width_here * lax.axis_size("fsdp")
    scaling = 1.0 / math.sqrt(HEAD_DIM)
    q_float = q_raw.astype(jnp.float32)
    k_float = k_raw.astype(jnp.float32)
    q_squares, k_squares = lax.psum(
        (jnp.sum(q_float * q_float, axis=1), jnp.sum(k_float * k_float, axis=1)), "fsdp"
    )
    q_inverse = lax.rsqrt(q_squares / inner_width + EPSILON)
    k_inverse = lax.rsqrt(k_squares / inner_width + EPSILON)
    cosine, signed_sine = rotation(positions, heads_here, HEAD_DIM)
    q_normed = q_float * q_inverse[:, None]
    k_normed = k_float * k_inverse[:, None]
    q_rot = rotate(q_normed, cosine, signed_sine, 1.0).astype(jnp.bfloat16)
    k_rot = rotate(k_normed, cosine, signed_sine, 1.0).astype(jnp.bfloat16)
    selector = (jnp.arange(modulation.shape[0]) == step_index[0]).astype(jnp.float32)
    gate_row = jnp.dot(selector, modulation, precision=lax.Precision.HIGHEST)
    gated_cot = (gate_row[None, :] * cotangent.astype(jnp.float32)).astype(jnp.bfloat16)
    attn_cot = lax.dot_general(
        gated_cot, out_weight, (((1,), (1,)), ((), ())), preferred_element_type=jnp.float32
    ).astype(jnp.bfloat16)
    q_heads = split_heads(q_rot)
    k_heads = split_heads(k_rot)
    v_heads = split_heads(values)
    cot_heads = split_heads(attn_cot)
    run_top = jnp.full((heads_here, tokens_here), NEG_LARGE, jnp.float32)
    key_piece = lax.all_gather(k_rot, "ctx", axis=0, tiled=True)
    value_piece = lax.all_gather(values, "ctx", axis=0, tiled=True)
    key_h = split_heads(key_piece)
    scores = (
        jnp.einsum("thd,shd->hts", q_heads, key_h, preferred_element_type=jnp.float32) * scaling
    )
    new_top = jnp.maximum(run_top, jnp.max(scores, axis=2))
    weights = jnp.exp(scores - new_top[:, :, None])
    grad_prob = jnp.einsum(
        "thd,shd->hts", cot_heads, split_heads(value_piece), preferred_element_type=jnp.float32
    )
    product = weights * grad_prob
    new_total = jnp.sum(weights, axis=2)
    new_weight = jnp.sum(product, axis=2)
    new_first = jnp.einsum(
        "hts,shd->htd", product.astype(jnp.bfloat16), key_h, preferred_element_type=jnp.float32
    )
    new_second = jnp.einsum(
        "hts,shd->htd", weights.astype(jnp.bfloat16), key_h, preferred_element_type=jnp.float32
    )
    state = (new_top, new_total, new_weight, new_first, new_second)
    run_top, run_total, run_weight, run_first, run_second = state
    log_total = run_top + jnp.log(run_total)
    row_delta = run_weight / run_total
    dq_acc = (run_first - row_delta[:, :, None] * run_second) / run_total[:, :, None]
    dq_normed = rotate(join_heads(dq_acc) * scaling, cosine, signed_sine, -1.0)
    q_part = jnp.sum(dq_normed * q_normed, axis=1)
    q_slope = lax.psum(q_part, "fsdp")
    lse_all, delta_all = (
        lax.all_gather(log_total, "ctx", axis=1, tiled=True),
        lax.all_gather(row_delta, "ctx", axis=1, tiled=True),
    )
    query_piece = lax.all_gather(q_rot, "ctx", axis=0, tiled=True)
    cot_piece = lax.all_gather(attn_cot, "ctx", axis=0, tiled=True)
    query_h = split_heads(query_piece)
    cot_h = split_heads(cot_piece)
    scores = (
        jnp.einsum("shd,thd->hst", query_h, k_heads, preferred_element_type=jnp.float32) * scaling
    )
    probs_full = jnp.exp(scores - lse_all[:, :, None])
    probs_low = probs_full.astype(jnp.bfloat16)
    value_acc = jnp.einsum("hst,shd->htd", probs_low, cot_h, preferred_element_type=jnp.float32)
    grad_prob = jnp.einsum("shd,thd->hst", cot_h, v_heads, preferred_element_type=jnp.float32)
    dscore = (probs_full * (grad_prob - delta_all[:, :, None])).astype(jnp.bfloat16)
    key_acc = jnp.einsum("hst,shd->htd", dscore, query_h, preferred_element_type=jnp.float32)
    key_acc, value_acc = (key_acc, value_acc)
    dk_normed = rotate(join_heads(key_acc) * scaling, cosine, signed_sine, -1.0)
    k_part = jnp.sum(dk_normed * k_normed, axis=1)
    k_slope = lax.psum(k_part, "fsdp")
    query_grad = (
        q_inverse[:, None] * (dq_normed - q_normed * (q_slope / inner_width)[:, None])
    ).astype(jnp.bfloat16)
    key_grad = (
        k_inverse[:, None] * (dk_normed - k_normed * (k_slope / inner_width)[:, None])
    ).astype(jnp.bfloat16)
    value_grad = join_heads(value_acc).astype(jnp.bfloat16)
    return (query_grad, key_grad, value_grad)


def solution(mesh):
    return jax.shard_map(
        shards,
        mesh=mesh,
        in_specs=(
            P("ctx", "fsdp"),
            P("ctx", "fsdp"),
            P("ctx", "fsdp"),
            P("ctx", None),
            P("ctx", None),
            P("fsdp", None),
            P(),
            P(),
        ),
        out_specs=(P("ctx", "fsdp"), P("ctx", "fsdp"), P("ctx", "fsdp")),
        check_vma=False,
    )
```

profile of v0, /device:TPU:1, one launch (start us, length us, event | category | flops | bytes accessed | tf_op | source)
XLA Modules:
  0.0 1284.4 jit_solution(7268370278710370640)
XLA Ops:
  7.2 1.2 copy.33
  8.5 1.1 copy.34
  9.7 9.8 all-reduce.1
  20.5 1.1 cosine_bitcast_fusion
  21.6 1.0 fusion.42
  22.7 1.7 copy.38
  26.4 6.1 fusion.23
  32.5 1.1 copy.37
  33.5 237.3 %all-gather.5.cloned.1.call-done = bf16[8192,640]{0,1:T(8,128)(2,1)} async-done(((bf16[128,640]{0,1:T(8,128)(2,1)}), bf16[8192,640]{0,1:T(8,128)(2,1)}) %all-gather.5.cloned.1.call-update) | async-done | bytes 10485776 | tf_op jit(solution)/shard_map/all_gather | solution.py:88
  270.8 13.9 %multiply_reduce_fusion = (f32[5,128]{1,0:T(8,128)S(1)}, f32[5,128,8192]{2,1,0:T(8,128)}) fusion(bf16[128,5,128]{0,2,1:T(8,128)(2,1)S(1)} %bitcast.115, bf16[8192,5,128]{0,2,1:T(8,128)(2,1)} %bitcast.102), kind=kOutput, calls=%fused_computation.3 | convolution fusion | flops 1352662400 | bytes 31623680 | tf_op jit(solution)/shard_map/thd,shd->hts/dot_general | solution.py:92
  284.7 9.3 fusion.2
  294.0 261.6 %all-gather.7.cloned.1.call-done = bf16[8192,640]{0,1:T(8,128)(2,1)} async-done(((bf16[128,640]{0,1:T(8,128)(2,1)}), bf16[8192,640]{0,1:T(8,128)(2,1)}) %all-gather.7.cloned.1.call-update) | async-done | bytes 10485776 | tf_op jit(solution)/shard_map/all_gather | solution.py:89
  555.6 16.0 %fusion.77 = (f32[5,128]{1,0:T(8,128)S(1)}, bf16[5,128,8192]{2,1,0:T(8,128)(2,1)}) fusion(bf16[128,5,128]{0,2,1:T(8,128)(2,1)S(1)} %bitcast.117, bf16[8192,5,128]{0,2,1:T(8,128)(2,1)} %bitcast.109, f32[5,128]{1,0:T(8,128)S(1)} %broadcast_maximum_fusion, f32[5,128,8192]{2,1,0:T(8,128)} %get-tuple-element.42), kind=kOutput, calls=%fused_computation.93 | convolution fusion | flops 1368391040 | bytes 42112000 | tf_op jit(solution)/shard_map/thd,shd->hts/dot_general | solution.py:96
  571.5 129.9 %all_gather.21 = f32[5,8192]{1,0:T(8,128)S(1)} all-gather(f32[5,128]{1,0:T(8,128)S(1)} %get-tuple-element.39), channel_id=1, replica_groups=mesh['ctx'=64,'fsdp'=4] {'ctx'}, dimensions={1}, use_global_device_ids=true | all-gather | bytes 166400 | tf_op jit(solution)/shard_map/all_gather | solution.py:117
  701.4 127.9 %all_gather.23 = f32[5,8192]{1,0:T(8,128)S(1)} all-gather(f32[5,128]{1,0:T(8,128)S(1)} %get-tuple-element.40), channel_id=1, replica_groups=mesh['ctx'=64,'fsdp'=4] {'ctx'}, dimensions={1}, use_global_device_ids=true | all-gather | bytes 166400 | tf_op jit(solution)/shard_map/all_gather | solution.py:118
  829.3 9.9 fusion.16
  839.2 12.4 fusion.36
  852.3 11.3 fusion.80
  863.6 297.1 %all-gather.11.cloned.1.call-done = bf16[8192,640]{1,0:T(8,128)(2,1)} async-done(((bf16[128,640]{1,0:T(8,128)(2,1)}), bf16[8192,640]{1,0:T(8,128)(2,1)}) %all-gather.11.cloned.1.call-update) | async-done | bytes 10485776 | tf_op jit(solution)/shard_map/all_gather | solution.py:121
  1160.7 14.3 %copy.43 = bf16[8192,640]{0,1:T(8,128)(2,1)} copy(bf16[8192,640]{1,0:T(8,128)(2,1)} %all-gather.11.cloned.1.call-done) | data formatting | bytes 20971520 | tf_op jit(solution)/shard_map/all_gather | solution.py:121
  1175.0 16.1 %fusion.24 = bf16[5,128,128]{1,2,0:T(8,128)(2,1)S(1)} fusion(bf16[8192,5,128]{0,2,1:T(8,128)(2,1)} %bitcast.105, f32[5,8192,128]{2,1,0:T(8,128)} %fusion.80, f32[5,8192]{1,0:T(8,128)S(1)} %all_gather.21), kind=kOutput, calls=%fused_computation.24 | convolution fusion | flops 1357987840 | bytes 31784960 | tf_op jit(solution)/shard_map/hst,shd->htd/dot_general | solution.py:129
  1191.1 2.9 copy-done.3
  1194.0 18.0 %multiply_convert_fusion.clone.6 = bf16[5,8192,128]{2,1,0:T(8,128)(2,1)} fusion(f32[5,8192,128]{2,1,0:T(8,128)S(1)} %copy-done.2, bf16[8192,5,128]{0,2,1:T(8,128)(2,1)S(1)} %bitcast.106, bf16[128,5,128]{0,2,1:T(8,128)(2,1)S(1)} %bitcast.116, f32[5,8192]{1,0:T(8,128)S(1)} %all_gather.23, f32[5,8192]{1,0:T(8,128)S(1)} %all_gather.21), kind=kOutput, calls=%fused_computation.clone.clone.clone.clone.clone.1 | convolution fusion | flops 1368391680 | bytes 42434560 | tf_op jit(solution)/shard_map/shd,thd->hst/dot_general | solution.py:130
  1212.0 9.9 fusion.22
  1221.9 0.8 fusion.69
  1222.6 0.8 copy.47
  1223.5 2.1 multiply_reduce_fusion.1
  1225.6 48.5 %all-reduce = (f32[128]{0:T(128)S(1)}, f32[128]{0:T(128)S(1)}) all-reduce(f32[128]{0:T(128)S(1)} %get-tuple-element.33, f32[128]{0:T(128)S(1)} %get-tuple-element.13), channel_id=1, replica_groups=mesh['ctx'=64,'fsdp'=4] {'fsdp'}, use_global_device_ids=true, to_apply=%region_8.9 | all-reduce | flops 256 | bytes 2048 | tf_op jit(solution)/shard_map/psum | solution.py:115
  1274.1 1.0 multiply_convert_fusion.6
  1275.1 0.8 copy.45
  1276.0 1.0 multiply_convert_fusion.5
  1277.0 0.8 copy.46
  (53 shorter events, 3.3 us)
Async XLA Ops:
  7.2 18.7 %copy-start = (f32[50,5120]{1,0:T(8,128)S(1)}, f32[50,5120]{1,0:T(8,128)}, u32[]{:S(2)}) copy-start(f32[50,5120]{1,0:T(8,128)} %param.16) | copy-start | bytes 3072004
  7.2 263.6 %all-gather.5.cloned.1.call-start = ((), (), s32[]{:S(2)}) async-start(), calls=%async_computation | async-start | bytes 10649600 | tf_op jit(solution)/shard_map/all_gather | solution.py:88
  21.6 263.1 %copy-start.7 = (f32[128,64,2]{0,2,1:T(2,128)}, f32[128,64,2]{0,2,1:T(2,128)S(1)}, u32[]{:S(2)}) copy-start(f32[128,64,2]{0,2,1:T(2,128)S(1)} %broadcast_in_dim.35) | copy-start | bytes 196612
  22.6 248.2 %copy-start.5 = (bf16[128,640]{0,1:T(8,128)(2,1)S(1)}, bf16[128,640]{0,1:T(8,128)(2,1)}, u32[]{:S(2)}) copy-start(bf16[128,640]{0,1:T(8,128)(2,1)} %get-tuple-element.35) | copy-start | bytes 491524
  22.7 532.9 %all-gather.7.cloned.1.call-start = ((), (), s32[]{:S(2)}) async-start(), calls=%async_computation.1 | async-start | bytes 10649600 | tf_op jit(solution)/shard_map/all_gather | solution.py:89
  24.4 827.8 %all-gather.9.cloned.1.call-start = ((), (), s32[]{:S(2)}) async-start(), calls=%async_computation.2 | async-start | bytes 10649600 | tf_op jit(solution)/shard_map/all_gather | solution.py:120
  25.2 1135.5 %all-gather.11.cloned.1.call-start = ((), (), s32[]{:S(2)}) async-start(), calls=%async_computation.3 | async-start | bytes 10649600 | tf_op jit(solution)/shard_map/all_gather | solution.py:121
  839.2 13.1 %copy-start.4 = (bf16[128,640]{0,1:T(8,128)(2,1)S(1)}, bf16[128,640]{0,1:T(8,128)(2,1)}, u32[]{:S(2)}) copy-start(bf16[128,640]{0,1:T(8,128)(2,1)} %get-tuple-element.36) | copy-start | bytes 491524
  1175.0 16.1 %copy-start.2 = (f32[5,8192,128]{2,1,0:T(8,128)S(1)}, f32[5,8192,128]{2,1,0:T(8,128)}, u32[]{:S(2)}) copy-start(f32[5,8192,128]{2,1,0:T(8,128)} %fusion.80) | copy-start | bytes 62914564
  1175.0 19.0 %copy-start.3 = (bf16[8192,640]{0,1:T(8,128)(2,1)S(1)}, bf16[8192,640]{0,1:T(8,128)(2,1)}, u32[]{:S(2)}) copy-start(bf16[8192,640]{0,1:T(8,128)(2,1)} %copy.43) | copy-start | bytes 31457284
  1175.0 19.0 %copy-start.6 = (bf16[128,640]{0,1:T(8,128)(2,1)S(1)}, bf16[128,640]{0,1:T(8,128)(2,1)}, u32[]{:S(2)}) copy-start(bf16[128,640]{0,1:T(8,128)(2,1)} %copy.38) | copy-start | bytes 491524
  1194.0 83.8 %copy-start.1 = (f32[50,5120]{1,0:T(8,128)S(1)}, f32[50,5120]{1,0:T(8,128)}, u32[]{:S(2)}) copy-start(f32[50,5120]{1,0:T(8,128)} %param.16) | copy-start | bytes 3072004
  1212.0 11.5 copy-start.8
  1212.0 11.5 copy-start.9
  1212.0 11.5 copy-start.10
Sparse Core Ops, SparseCore 0:
  22.8 247.9 all-gather.4
  272.5 283.0 all-gather.6
  557.8 284.7 all-gather.8
  844.8 315.8 all-gather.10
where the time goes:
time: 1290 us; the launch traced here: 1280 us
  waiting for transfers between devices  797 us (62%)
  blocking collectives  316 us (24%)
  matrix products  115 us (9%)
  local copies, waits for them, and re-layouts  27 us (2%)
  other arithmetic  14.9 us (1%)
  between operations  14.6 us (1%)
    all_gather x1, waiting for transfers between devices, shards(): cot_piece = lax.all_gather(attn_cot, 'ctx', axis=0, tiled=True)  297 us
    all_gather x1, waiting for transfers between devices, shards(): value_piece = lax.all_gather(values, 'ctx', axis=0, tiled=True)  262 us
    all_gather x1, waiting for transfers between devices, shards(): key_piece = lax.all_gather(k_rot, 'ctx', axis=0, tiled=True)  237 us
    all_gather x1, blocking collectives, shards(): lax.all_gather(log_total, 'ctx', axis=1, tiled=True)  130 us
    all_gather x1, blocking collectives, shards(): lax.all_gather(row_delta, 'ctx', axis=1, tiled=True)  128 us
    psum x1, blocking collectives, shards(): q_slope = lax.psum(q_part, 'fsdp')  48.5 us
  transfers between devices with their start and end apart: 4, of which 3 were waited for; matrix products, arithmetic and copies ran while one was open for 6% of the time, Pallas kernels for 0%

commit v1 on v0

v1 whole, which is shorter than its diff:
```python
import math

import jax
import jax.numpy as jnp
import numpy as np
from jax import lax
from jax.experimental import pallas as pl
from jax.experimental.pallas import tpu as pltpu
from jax.sharding import Mesh
from jax.sharding import PartitionSpec as P

HEAD_DIM = 128
EPSILON = 1e-06
LOG2E = math.log2(math.e)
SCALING = 1.0 / math.sqrt(HEAD_DIM)
TOKENS_AXES = ("xl", "z", "y")
HEADS_AXES = ("xh", "c")
VMEM_LIMIT = 48 * 1024 * 1024
NT = (((1,), (1,)), ((), ()))
TN = (((0,), (0,)), ((), ()))


def angle_table(head_size):
    side_dim = 2 * (head_size // 6)
    first_dim = head_size - 2 * side_dim
    freq_table = np.zeros((3, head_size // 2), np.float32)
    column = 0
    for axis_number, group_dim in enumerate([first_dim, side_dim, side_dim]):
        for pair_index in range(group_dim // 2):
            freq_table[axis_number, column] = 10000.0 ** (-2.0 * pair_index / group_dim)
            column += 1
    return freq_table


def rotation(positions, heads_count):
    angles = jnp.dot(
        positions.astype(jnp.float32),
        jnp.asarray(np.repeat(angle_table(HEAD_DIM), 2, axis=1)),
        precision=lax.Precision.HIGHEST,
    )
    parity = jnp.tile(jnp.array([-1.0, 1.0], jnp.float32), HEAD_DIM // 2)
    cosine = jnp.cos(angles)
    signed_sine = jnp.sin(angles) * parity[None, :]
    return jnp.tile(cosine, (1, heads_count)), jnp.tile(signed_sine, (1, heads_count))


def rotate(source, cosine, signed_sine, direction):
    column_ids = jnp.arange(source.shape[1])
    partner = jnp.where(
        column_ids % 2 == 0, jnp.roll(source, -1, axis=1), jnp.roll(source, 1, axis=1)
    )
    return source * cosine + direction * partner * signed_sine


def shift(x, axis, distance):
    size = lax.axis_size(axis)
    return lax.ppermute(x, axis, [(i, (i + distance) % size) for i in range(size)])


def swap_core(x):
    return lax.ppermute(x, ("xl", "c"), [(0, 0), (1, 2), (2, 1), (3, 3)])


def blocks_of(refs, column):
    return jnp.concatenate([ref[:, pl.ds(column, HEAD_DIM)] for ref in refs], axis=0)


def stats_kernel(nq, nk, heads, *refs):
    query_refs, key_refs = refs[:nq], refs[nq : nq + nk]
    stats_ref, k_ref, v_ref = refs[nq + nk :]
    width = heads * HEAD_DIM
    stats_ref[...] = jnp.zeros_like(stats_ref)

    @pl.loop(0, heads)
    def _(h):
        col = pl.multiple_of(h * HEAD_DIM, HEAD_DIM)
        cot_col = pl.multiple_of(width + h * HEAD_DIM, HEAD_DIM)
        k_ref[...] = blocks_of(key_refs, col)
        v_ref[...] = blocks_of(key_refs, cot_col)
        for t in range(nq // 2):
            pair = query_refs[2 * t : 2 * t + 2]
            q = blocks_of(pair, col)
            cot = blocks_of(pair, cot_col)
            s = lax.dot_general(k_ref[...], q, NT, preferred_element_type=jnp.float32)
            g = lax.dot_general(v_ref[...], cot, NT, preferred_element_type=jnp.float32)
            s = s * (SCALING * LOG2E)
            top = jnp.max(s, axis=0, keepdims=True)
            e = jnp.exp2(s - top)
            cols = slice(t * 256, t * 256 + 256)
            stats_ref[pl.ds(h, 1), cols] = top
            stats_ref[pl.ds(8 + h, 1), cols] = jnp.sum(e, axis=0, keepdims=True)
            stats_ref[pl.ds(16 + h, 1), cols] = jnp.sum(e * g, axis=0, keepdims=True)


def grads_kernel(nq, nk, heads, *refs):
    query_refs, key_refs = refs[:nq], refs[nq : nq + nk]
    totals_ref = refs[nq + nk]
    outs = refs[nq + nk + 1 :]
    dq_refs, mine_ref, other_ref = outs[:nq], outs[nq], outs[nq + 1]
    k_ref, v_ref, dk_ref, dv_ref = outs[nq + 2 :]
    width = heads * HEAD_DIM
    half = nk // 2 * 128

    @pl.loop(0, heads)
    def _(h):
        col = pl.multiple_of(h * HEAD_DIM, HEAD_DIM)
        cot_col = pl.multiple_of(width + h * HEAD_DIM, HEAD_DIM)
        k_ref[...] = blocks_of(key_refs, col)
        v_ref[...] = blocks_of(key_refs, cot_col)
        for t in range(nq // 2):
            pair = query_refs[2 * t : 2 * t + 2]
            q = blocks_of(pair, col)
            cot = blocks_of(pair, cot_col)
            cols = slice(t * 256, t * 256 + 256)
            log_total = totals_ref[pl.ds(h, 1), cols]
            delta = totals_ref[pl.ds(8 + h, 1), cols]
            s = lax.dot_general(k_ref[...], q, NT, preferred_element_type=jnp.float32)
            g = lax.dot_general(v_ref[...], cot, NT, preferred_element_type=jnp.float32)
            p = jnp.exp2(s * (SCALING * LOG2E) - log_total)
            ds = (p * (g - delta)).astype(jnp.bfloat16)
            dv = jnp.dot(p.astype(jnp.bfloat16), cot, preferred_element_type=jnp.float32)
            dk = jnp.dot(ds, q, preferred_element_type=jnp.float32)
            if t == 0:
                dv_ref[...] = dv
                dk_ref[...] = dk
            else:
                dv_ref[...] += dv
                dk_ref[...] += dk
            dq = lax.dot_general(ds, k_ref[...], TN, preferred_element_type=jnp.float32)
            dq = (dq * SCALING).astype(jnp.bfloat16)
            dq_refs[2 * t][:, pl.ds(col, HEAD_DIM)] = dq[:128]
            dq_refs[2 * t + 1][:, pl.ds(col, HEAD_DIM)] = dq[128:]
        dk = (dk_ref[...] * SCALING).astype(jnp.bfloat16)
        dv = dv_ref[...].astype(jnp.bfloat16)
        mine_ref[:, pl.ds(col, HEAD_DIM)] = dk[:half]
        other_ref[:, pl.ds(col, HEAD_DIM)] = dk[half:]
        mine_ref[:, pl.ds(cot_col, HEAD_DIM)] = dv[:half]
        other_ref[:, pl.ds(cot_col, HEAD_DIM)] = dv[half:]


def block_stats(queries, keys, heads):
    nq, nk = len(queries), len(keys)
    vmem = pl.BlockSpec(memory_space=pltpu.VMEM)
    return pl.pallas_call(
        lambda *refs: stats_kernel(nq, nk, heads, *refs),
        out_shape=jax.ShapeDtypeStruct((24, nq * 128), jnp.float32),
        in_specs=[vmem] * (nq + nk),
        out_specs=vmem,
        scratch_shapes=[
            pltpu.VMEM((nk * 128, HEAD_DIM), jnp.bfloat16),
            pltpu.VMEM((nk * 128, HEAD_DIM), jnp.bfloat16),
        ],
        compiler_params=pltpu.CompilerParams(vmem_limit_bytes=VMEM_LIMIT),
        cost_estimate=pl.CostEstimate(
            flops=heads * nq * nk * 128 * 128 * 128 * 4,
            bytes_accessed=(nq + nk) * 128 * heads * 512,
            transcendentals=heads * nq * nk * 128 * 128,
        ),
        name="block_stats",
    )(*queries, *keys)


def block_grads(queries, keys, totals, heads):
    nq, nk = len(queries), len(keys)
    width = heads * HEAD_DIM
    vmem = pl.BlockSpec(memory_space=pltpu.VMEM)
    outs = pl.pallas_call(
        lambda *refs: grads_kernel(nq, nk, heads, *refs),
        out_shape=[jax.ShapeDtypeStruct((128, width), jnp.bfloat16)] * nq
        + [jax.ShapeDtypeStruct((nk // 2 * 128, 2 * width), jnp.bfloat16)] * 2,
        in_specs=[vmem] * (nq + nk + 1),
        out_specs=[vmem] * (nq + 2),
        scratch_shapes=[
            pltpu.VMEM((nk * 128, HEAD_DIM), jnp.bfloat16),
            pltpu.VMEM((nk * 128, HEAD_DIM), jnp.bfloat16),
            pltpu.VMEM((nk * 128, HEAD_DIM), jnp.float32),
            pltpu.VMEM((nk * 128, HEAD_DIM), jnp.float32),
        ],
        compiler_params=pltpu.CompilerParams(vmem_limit_bytes=VMEM_LIMIT),
        cost_estimate=pl.CostEstimate(
            flops=heads * nq * nk * 128 * 128 * 128 * 10,
            bytes_accessed=(nq + nk) * 128 * heads * 1024,
            transcendentals=heads * nq * nk * 128 * 128,
        ),
        name="block_grads",
    )(*queries, *keys, totals)
    return outs[:nq], outs[nq], outs[nq + 1]


def shift_stats(stats, distance):
    moved = shift(stats, "z", distance)
    return jnp.roll(moved, distance * 128, axis=1)


def merge(parts):
    top = parts[0][:8]
    for part in parts[1:]:
        top = jnp.maximum(top, part[:8])
    total = weight = 0.0
    for part in parts:
        factor = jnp.exp2(part[:8] - top)
        total = total + part[8:16] * factor
        weight = weight + part[16:] * factor
    return top, total, weight


def shards(q_raw, k_raw, values, positions, cotangent, out_weight, modulation, step_index):
    width = q_raw.shape[1]
    heads = width // HEAD_DIM
    inner_width = width * 4
    q_float = q_raw.astype(jnp.float32)
    k_float = k_raw.astype(jnp.float32)
    squares = jnp.stack(
        [jnp.sum(q_float * q_float, axis=1), jnp.sum(k_float * k_float, axis=1)]
    )
    squares = squares + shift(squares, "c", 1)
    squares = squares + shift(squares, "xh", 1)
    inverse = lax.rsqrt(squares / inner_width + EPSILON)
    gate_row = lax.dynamic_slice_in_dim(modulation, step_index[0], 1, 0)
    gated_cot = (gate_row * cotangent.astype(jnp.float32)).astype(jnp.bfloat16)
    attn_cot = lax.dot_general(
        gated_cot, out_weight, NT, preferred_element_type=jnp.float32
    ).astype(jnp.bfloat16)
    cosine, signed_sine = rotation(positions, heads)
    q_normed = q_float * inverse[0][:, None]
    k_normed = k_float * inverse[1][:, None]
    q_rot = rotate(q_normed, cosine, signed_sine, 1.0).astype(jnp.bfloat16)
    k_rot = rotate(k_normed, cosine, signed_sine, 1.0).astype(jnp.bfloat16)

    query_own = swap_core(jnp.concatenate([q_rot, attn_cot], axis=1))
    key_own = swap_core(jnp.concatenate([k_rot, values], axis=1))

    left, right = query_own, query_own
    from_left, from_right = [], []
    for _ in range(3):
        left, right = shift(left, "z", 1), shift(right, "z", -1)
        from_left.append(left)
        from_right.append(right)
    far = jnp.concatenate([shift(left[:64], "z", 1), shift(right[64:], "z", -1)], axis=0)
    queries = [query_own, *from_left, far, *from_right[::-1]]

    keys = [key_own] + [shift(key_own, "y", d) for d in (1, 2, 3)]
    keys = keys + [shift(block, "c", 1) for block in keys]

    stats = block_stats(queries, keys, heads)
    stats = jnp.concatenate(merge([stats, shift_stats(stats, 1)]), axis=0)
    top, total, weight = merge([stats] + [shift_stats(stats, d) for d in (2, -2, 4)])
    valid = jnp.arange(8)[:, None] < heads
    total = jnp.where(valid, total, 1.0)
    totals = jnp.concatenate([top + jnp.log2(total), weight / total], axis=0)

    dq, mine, other = block_grads(queries, keys, totals, heads)

    left, right = shift(dq[4][:64], "z", -1), shift(dq[4][64:], "z", 1)
    left = dq[3] + jnp.concatenate([left, jnp.zeros_like(left)], axis=0)
    right = dq[5] + jnp.concatenate([jnp.zeros_like(right), right], axis=0)
    left = dq[2] + shift(left, "z", -1)
    right = dq[6] + shift(right, "z", 1)
    left = dq[1] + shift(left, "z", -1)
    right = dq[7] + shift(right, "z", 1)
    f32 = jnp.float32
    dq_sum = dq[0].astype(f32) + shift(left, "z", -1).astype(f32) + shift(right, "z", 1).astype(f32)

    chip_sum = (mine.astype(f32) + shift(other, "c", 1).astype(f32)).astype(jnp.bfloat16)
    dkv_sum = chip_sum[:128].astype(f32)
    for d in (1, 2, 3):
        dkv_sum = dkv_sum + shift(chip_sum[128 * d : 128 * d + 128], "y", -d).astype(f32)

    slopes = jnp.stack(
        [
            jnp.sum(dq_sum * query_own[:, :width].astype(f32), axis=1),
            jnp.sum(dkv_sum[:, :width] * key_own[:, :width].astype(f32), axis=1),
        ]
    )
    slope_sum = 0.0
    for a in (0, 1):
        for b in (0, 1):
            perm = [
                (xl * 4 + xh * 2 + c, c * 4 + (xh ^ b) * 2 + (xl ^ a))
                for xl in (0, 1)
                for xh in (0, 1)
                for c in (0, 1)
            ]
            slope_sum = slope_sum + lax.ppermute(slopes, ("xl", "xh", "c"), perm)
    slope = slope_sum / inner_width

    packed = jnp.concatenate([dq_sum, dkv_sum], axis=1).astype(jnp.bfloat16)
    packed = swap_core(packed)
    dq_normed = rotate(packed[:, :width].astype(f32), cosine, signed_sine, -1.0)
    dk_normed = rotate(packed[:, width : 2 * width].astype(f32), cosine, signed_sine, -1.0)
    query_grad = inverse[0][:, None] * (dq_normed - q_normed * slope[0][:, None])
    key_grad = inverse[1][:, None] * (dk_normed - k_normed * slope[1][:, None])
    return (
        query_grad.astype(jnp.bfloat16),
        key_grad.astype(jnp.bfloat16),
        packed[:, 2 * width :],
    )


def solution(mesh):
    axes = ("xl", "z", "y", "xh", "c")
    fine = Mesh(np.asarray(mesh.devices).reshape(2, 8, 4, 2, 2), axes)
    split = P(TOKENS_AXES, HEADS_AXES)
    rows = P(TOKENS_AXES, None)
    return jax.shard_map(
        shards,
        mesh=fine,
        in_specs=(split, split, split, rows, rows, P(HEADS_AXES, None), P(), P()),
        out_specs=(split, split, split),
        check_vma=False,
    )
```

time: 1290 us -> 171 us (0.13)
  waiting for transfers between devices: 797 us -> 63.7 us
  blocking collectives: 316 us -> 0 us
  matrix products: 115 us -> 5.92 us
  starting transfers between devices: 0.16 us -> 63.9 us
  Pallas kernels: 0 us -> 26.9 us
  local copies, waits for them, and re-layouts: 27 us -> 2.37 us
    all_gather x4 -> x0, waiting for transfers between devices: 796 us -> none  [the longest x1 297 us: shards(): cot_piece = lax.all_gather(attn_cot, 'ctx', axis=0, tiled=True)]
    all_gather x2 -> x0, blocking collectives: 258 us -> none  [the longest x1 130 us: shards(): lax.all_gather(log_total, 'ctx', axis=1, tiled=True)]
    dot_general x11 -> x2, matrix products: 115 us -> 5.92 us  [the longest x1 5.4 us: shards(): lax.dot_general(gated_cot, out_weight, NT, preferred_element_type=jnp.flo...]
    ppermute x0 -> x40, starting transfers between devices: none -> 63.9 us  [the longest x33 42.6 us: shift(): lax.ppermute(x, axis, [(i, (i + distance) % size) for i in range(size)])]
    ppermute x0 -> x40, waiting for transfers between devices: none -> 63.7 us  [the longest x33 55.1 us: shift(): lax.ppermute(x, axis, [(i, (i + distance) % size) for i in range(size)])]
    psum x2 -> x0, blocking collectives: 58.3 us -> none  [the longest x1 48.5 us: shards(): q_slope = lax.psum(q_part, 'fsdp')]
    pallas_call x0 -> x2, Pallas kernels: none -> 26.9 us  [the longest x1 17.3 us: block_grads(): pl.pallas_call(lambda *refs: grads_kernel(nq, nk, heads, *refs), out_shap...]
    all_gather x1 -> x0, local copies, waits for them, and re-layouts: 14.3 us -> none  [shards(): cot_piece = lax.all_gather(attn_cot, 'ctx', axis=0, tiled=True)]
  transfers between devices with their start and end apart: 4 -> 40, of which waited for: 3 -> 19; matrix products, arithmetic and copies ran while one was open for 6% -> 5% of each run, Pallas kernels for 0% -> 0%
where the time goes in v1:
time: 171 us
  starting transfers between devices  63.9 us (37%)
  waiting for transfers between devices  63.7 us (37%)
  Pallas kernels  26.9 us (16%)
  matrix products  5.92 us (3%)
  other arithmetic  5.86 us (3%)
  local copies, waits for them, and re-layouts  2.37 us (1%)
  between operations  1.86 us (1%)
    ppermute x33, waiting for transfers between devices, shift(): lax.ppermute(x, axis, [(i, (i + distance) % size) for i in range(size)])  55.1 us
    ppermute x33, starting transfers between devices, shift(): lax.ppermute(x, axis, [(i, (i + distance) % size) for i in range(size)])  42.6 us
    pallas_call x1, Pallas kernels, block_grads(): pl.pallas_call(lambda *refs: grads_kernel(nq, nk, heads, *refs), out_shap...  17.3 us
    ppermute x3, starting transfers between devices, swap_core(): return lax.ppermute(x, ('xl', 'c'), [(0, 0), (1, 2), (2, 1), (3, 3)])  14.8 us
    pallas_call x1, Pallas kernels, block_stats(): pl.pallas_call(lambda *refs: stats_kernel(nq, nk, heads, *refs), out_shap...  9.6 us
    ppermute x4, starting transfers between devices, shards(): slope_sum = slope_sum + lax.ppermute(slopes, ('xl', 'xh', 'c'), perm)  6.44 us
    ppermute x3, waiting for transfers between devices, swap_core(): return lax.ppermute(x, ('xl', 'c'), [(0, 0), (1, 2), (2, 1), (3, 3)])  6.26 us
    dot_general x1, matrix products, shards(): lax.dot_general(gated_cot, out_weight, NT, preferred_element_type=jnp.flo...  5.4 us
  transfers between devices with their start and end apart: 40, of which 19 were waited for; matrix products, arithmetic and copies ran while one was open for 5% of the time, Pallas kernels for 0%

profile of v1, /device:TPU:1, one launch (start us, length us, event | category | flops | bytes accessed | tf_op | source)
XLA Modules:
  0.0 170.5 jit_solution(16220385777598481124)
XLA Ops:
  2.8 3.3 %collective-permute-start = (f32[2,128]{1,0:T(2,128)S(1)}, f32[2,128]{1,0:T(2,128)S(1)}, u32[]{:S(2)}, u32[]{:S(2)}) collective-permute-start(f32[2,128]{1,0:T(2,128)S(1)} %pad_maximum_fusion.9), channel_id=1, source_target_pairs={{0,1},{1,0},{2,3},{3,2},{4,5},{5,4},{6,7},{7,6},{8,9},{9,8},{10,11... | collective-permute-start | bytes 3080 | tf_op jit(solution)/shard_map/ppermute | solution.py:57
  7.7 5.4 %fusion.2 = bf16[128,640]{1,0:T(8,128)(2,1)S(1)} fusion(bf16[640,5120]{1,0:T(8,128)(2,1)} %param.15, bf16[128,5120]{1,0:T(8,128)(2,1)} %param.14, f32[5120]{0:T(1024)S(1)} %bitcast.27), kind=kOutput, calls=%fused_computation.4 | convolution fusion | flops 840908800 | bytes 8048640 | tf_op jit(solution)/shard_map/dot_general | solution.py:221
  15.2 2.5 %collective-permute-done.1 = f32[2,128]{1,0:T(2,128)S(1)} collective-permute-done((f32[2,128]{1,0:T(2,128)S(1)}, f32[2,128]{1,0:T(2,128)S(1)}, u32[]{:S(2)}, u32[]{:S(2)}) %collective-permute-start.1) | collective-permute-done | bytes 1056 | tf_op jit(solution)/shard_map/ppermute | solution.py:57
  18.8 2.4 %collective-permute-start.2 = (bf16[128,1280]{1,0:T(8,128)(2,1)S(1)}, bf16[128,1280]{1,0:T(8,128)(2,1)S(1)}, u32[]{:S(2)}, u32[]{:S(2)}) collective-permute-start(bf16[128,1280]{1,0:T(8,128)(2,1)S(1)} %pad_maximum_fusion.1), channel_id=1, source_target_pairs={{0,0},{1,128},{128,1},{129,129},{2,2},{3,130},{130,3},{131,131},{4... | collective-permute-start | bytes 983048 | tf_op jit(solution)/shard_map/ppermute | solution.py:61
  21.2 6.3 %collective-permute-done.2.refs_0_ = bf16[128,1280]{1,0:T(8,128)(2,1)S(1)} collective-permute-done((bf16[128,1280]{1,0:T(8,128)(2,1)S(1)}, bf16[128,1280]{1,0:T(8,128)(2,1)S(1)}, u32[]{:S(2)}, u32[]{:S(2)}) %collective-permute-start.2) | collective-permute-done | bytes 327712 | tf_op jit(solution)/shard_map/ppermute | solution.py:61
  27.9 3.9 %collective-permute-start.7 = (bf16[128,1280]{1,0:T(8,128)(2,1)S(1)}, bf16[128,1280]{1,0:T(8,128)(2,1)S(1)}, u32[]{:S(2)}, u32[]{:S(2)}) collective-permute-start(bf16[128,1280]{1,0:T(8,128)(2,1)S(1)} %collective-permute-done.2.refs_0_), channel_id=1, source_target_pairs={{0,112},{16,0},{32,16},{48,32},{64,48},{80,64},{96,80},{112,96},{1... | collective-permute-start | bytes 983048 | tf_op jit(solution)/shard_map/ppermute | solution.py:57
  31.8 7.0 %collective-permute-done.3.refs_1_ = bf16[128,1280]{1,0:T(8,128)(2,1)S(1)} collective-permute-done((bf16[128,1280]{1,0:T(8,128)(2,1)S(1)}, bf16[128,1280]{1,0:T(8,128)(2,1)S(1)}, u32[]{:S(2)}, u32[]{:S(2)}) %collective-permute-start.3) | collective-permute-done | bytes 327712 | tf_op jit(solution)/shard_map/ppermute | solution.py:57
  38.9 3.3 %collective-permute-start.11 = (bf16[128,1280]{1,0:T(8,128)(2,1)S(1)}, bf16[128,1280]{1,0:T(8,128)(2,1)S(1)}, u32[]{:S(2)}, u32[]{:S(2)}) collective-permute-start(bf16[128,1280]{1,0:T(8,128)(2,1)S(1)} %pad_maximum_fusion.2), channel_id=1, source_target_pairs={{0,0},{1,128},{128,1},{129,129},{2,2},{3,130},{130,3},{131,131},{4... | collective-permute-start | bytes 983048 | tf_op jit(solution)/shard_map/ppermute | solution.py:61
  42.2 3.0 %collective-permute-start.8 = (bf16[128,1280]{1,0:T(8,128)(2,1)S(1)}, bf16[128,1280]{1,0:T(8,128)(2,1)S(1)}, u32[]{:S(2)}, u32[]{:S(2)}) collective-permute-start(bf16[128,1280]{1,0:T(8,128)(2,1)S(1)} %collective-permute-done.7.refs_7_), channel_id=1, source_target_pairs={{0,112},{16,0},{32,16},{48,32},{64,48},{80,64},{96,80},{112,96},{1... | collective-permute-start | bytes 983048 | tf_op jit(solution)/shard_map/ppermute | solution.py:57
  45.3 2.4 %collective-permute-done.4.refs_2_ = bf16[128,1280]{1,0:T(8,128)(2,1)S(1)} collective-permute-done((bf16[128,1280]{1,0:T(8,128)(2,1)S(1)}, bf16[128,1280]{1,0:T(8,128)(2,1)S(1)}, u32[]{:S(2)}, u32[]{:S(2)}) %collective-permute-start.4) | collective-permute-done | bytes 327712 | tf_op jit(solution)/shard_map/ppermute | solution.py:57
  47.6 2.7 %collective-permute-start.14 = (bf16[128,1280]{1,0:T(8,128)(2,1)S(1)}, bf16[128,1280]{1,0:T(8,128)(2,1)S(1)}, u32[]{:S(2)}, u32[]{:S(2)}) collective-permute-start(bf16[128,1280]{1,0:T(8,128)(2,1)S(1)} %collective-permute-done.11.refs_8_), channel_id=1, source_target_pairs={{0,12},{4,0},{8,4},{12,8},{1,13},{5,1},{9,5},{13,9},{2,14},{6,2},{... | collective-permute-start | bytes 983048 | tf_op jit(solution)/shard_map/ppermute | solution.py:57
  51.4 2.7 %collective-permute-start.9 = (bf16[128,1280]{1,0:T(8,128)(2,1)S(1)}, bf16[128,1280]{1,0:T(8,128)(2,1)S(1)}, u32[]{:S(2)}, u32[]{:S(2)}) collective-permute-start(bf16[128,1280]{1,0:T(8,128)(2,1)S(1)} %collective-permute-done.8.refs_6_), channel_id=1, source_target_pairs={{0,112},{16,0},{32,16},{48,32},{64,48},{80,64},{96,80},{112,96},{1... | collective-permute-start | bytes 983048 | tf_op jit(solution)/shard_map/ppermute | solution.py:57
  55.5 2.7 %collective-permute-done.14.refs_11_ = bf16[128,1280]{1,0:T(8,128)(2,1)S(1)} collective-permute-done((bf16[128,1280]{1,0:T(8,128)(2,1)S(1)}, bf16[128,1280]{1,0:T(8,128)(2,1)S(1)}, u32[]{:S(2)}, u32[]{:S(2)}) %collective-permute-start.14) | collective-permute-done | bytes 327712 | tf_op jit(solution)/shard_map/ppermute | solution.py:57
  58.7 3.2 %collective-permute-done.12.refs_9_ = bf16[128,1280]{1,0:T(8,128)(2,1)S(1)} collective-permute-done((bf16[128,1280]{1,0:T(8,128)(2,1)S(1)}, bf16[128,1280]{1,0:T(8,128)(2,1)S(1)}, u32[]{:S(2)}, u32[]{:S(2)}) %collective-permute-start.12) | collective-permute-done | bytes 327712 | tf_op jit(solution)/shard_map/ppermute | solution.py:57
  62.5 3.0 %collective-permute-start.10 = (bf16[64,1280]{1,0:T(8,128)(2,1)S(1)}, bf16[64,1280]{1,0:T(8,128)(2,1)S(1)}, u32[]{:S(2)}, u32[]{:S(2)}) collective-permute-start(bf16[64,1280]{1,0:T(8,128)(2,1)S(1)} %slice.252), channel_id=1, source_target_pairs={{0,112},{16,0},{32,16},{48,32},{64,48},{80,64},{96,80},{112,96},{1... | collective-permute-start | bytes 491528 | tf_op jit(solution)/shard_map/ppermute | solution.py:57
  65.5 3.6 %collective-permute-done.10 = bf16[64,1280]{1,0:T(8,128)(2,1)S(1)} collective-permute-done((bf16[64,1280]{1,0:T(8,128)(2,1)S(1)}, bf16[64,1280]{1,0:T(8,128)(2,1)S(1)}, u32[]{:S(2)}, u32[]{:S(2)}) %collective-permute-start.10) | collective-permute-done | bytes 163872 | tf_op jit(solution)/shard_map/ppermute | solution.py:57
  69.2 9.6 %block_stats.1 = f32[24,1024]{1,0:T(8,128)S(1)} custom-call(bf16[128,1280]{1,0:T(8,128)(2,1)S(1)} %collective-permute-done.2.refs_0_, bf16[128,1280]{1,0:T(8,128)(2,1)S(1)} %collective-permute-done.3.refs_1_, bf16[128,1280]{1,0:T(8,128)(2,1)S(1)} %collective-permute-done.4.refs_2_, bf16[128,1280]{1,0:T(8,128)(2,1)S(1)} %collective-permute-done.5.refs_3_, ...), custom_call_target="tpu_custom_call" | custom-call | flops 2684354560 | bytes 5242880 | tf_op jit(solution)/shard_map/block_stats/pallas_call | solution.py:144
  78.9 5.8 %collective-permute-done.19 = f32[24,1024]{1,0:T(8,128)S(1)} collective-permute-done((f32[24,1024]{1,0:T(8,128)S(1)}, f32[24,1024]{1,0:T(8,128)S(1)}, u32[]{:S(2)}, u32[]{:S(2)}) %collective-permute-start.19) | collective-permute-done | bytes 98336 | tf_op jit(solution)/shard_map/ppermute | solution.py:57
  84.8 4.1 %collective-permute-start.22 = (f32[24,1024]{1,0:T(8,128)S(1)}, f32[24,1024]{1,0:T(8,128)S(1)}, u32[]{:S(2)}, u32[]{:S(2)}) collective-permute-start(f32[24,1024]{1,0:T(8,128)S(1)} %pad_maximum_fusion.3), channel_id=1, source_target_pairs={{0,64},{16,80},{32,96},{48,112},{64,0},{80,16},{96,32},{112,48},{1... | collective-permute-start | bytes 294920 | tf_op jit(solution)/shard_map/ppermute | solution.py:57
  91.3 7.0 %collective-permute-done.21 = f32[24,1024]{1,0:T(8,128)S(1)} collective-permute-done((f32[24,1024]{1,0:T(8,128)S(1)}, f32[24,1024]{1,0:T(8,128)S(1)}, u32[]{:S(2)}, u32[]{:S(2)}) %collective-permute-start.21) | collective-permute-done | bytes 98336 | tf_op jit(solution)/shard_map/ppermute | solution.py:57
  98.5 17.3 %block_grads.1 = (bf16[128,640]{1,0:T(8,128)(2,1)S(1)}, bf16[128,640]{1,0:T(8,128)(2,1)S(1)}, bf16[128,640]{1,0:T(8,128)(2,1)S(1)}, bf16[128,640]{1,0:T(8,128)(2...) custom-call(bf16[128,1280]{1,0:T(8,128)(2,1)S(1)} %collective-permut, ...), custom_call_target="tpu_custom_call" | custom-call | flops 6710886400 | bytes 10485760 | tf_op jit(solution)/shard_map/block_grads/pallas_call | solution.py:167
  116.8 2.3 %collective-permute-start.27 = (bf16[64,640]{1,0:T(8,128)(2,1)S(1)}, bf16[64,640]{1,0:T(8,128)(2,1)S(1)}, u32[]{:S(2)}, u32[]{:S(2)}) collective-permute-start(bf16[64,640]{1,0:T(8,128)(2,1)S(1)} %get-tuple-element.58), channel_id=1, source_target_pairs={{0,16},{16,32},{32,48},{48,64},{64,80},{80,96},{96,112},{112,0},{1... | collective-permute-start | bytes 245768 | tf_op jit(solution)/shard_map/ppermute | solution.py:57
  119.6 2.6 %collective-permute-done.27 = bf16[64,640]{1,0:T(8,128)(2,1)S(1)} collective-permute-done((bf16[64,640]{1,0:T(8,128)(2,1)S(1)}, bf16[64,640]{1,0:T(8,128)(2,1)S(1)}, u32[]{:S(2)}, u32[]{:S(2)}) %collective-permute-start.27) | collective-permute-done | bytes 81952 | tf_op jit(solution)/shard_map/ppermute | solution.py:57
  125.1 3.4 %collective-permute-done.28 = bf16[128,640]{1,0:T(8,128)(2,1)S(1)} collective-permute-done((bf16[128,640]{1,0:T(8,128)(2,1)S(1)}, bf16[128,640]{1,0:T(8,128)(2,1)S(1)}, u32[]{:S(2)}, u32[]{:S(2)}) %collective-permute-start.28) | collective-permute-done | bytes 163872 | tf_op jit(solution)/shard_map/ppermute | solution.py:57
  128.6 2.7 %collective-permute-start.25 = (bf16[128,640]{1,0:T(8,128)(2,1)S(1)}, bf16[128,640]{1,0:T(8,128)(2,1)S(1)}, u32[]{:S(2)}, u32[]{:S(2)}) collective-permute-start(bf16[128,640]{1,0:T(8,128)(2,1)S(1)} %add.139), channel_id=1, source_target_pairs={{0,112},{16,0},{32,16},{48,32},{64,48},{80,64},{96,80},{112,96},{1... | collective-permute-start | bytes 491528 | tf_op jit(solution)/shard_map/ppermute | solution.py:57
  131.4 2.6 %collective-permute-done.29 = bf16[128,640]{1,0:T(8,128)(2,1)S(1)} collective-permute-done((bf16[128,640]{1,0:T(8,128)(2,1)S(1)}, bf16[128,640]{1,0:T(8,128)(2,1)S(1)}, u32[]{:S(2)}, u32[]{:S(2)}) %collective-permute-start.29) | collective-permute-done | bytes 163872 | tf_op jit(solution)/shard_map/ppermute | solution.py:57
  134.1 2.7 %collective-permute-start.26 = (bf16[128,640]{1,0:T(8,128)(2,1)S(1)}, bf16[128,640]{1,0:T(8,128)(2,1)S(1)}, u32[]{:S(2)}, u32[]{:S(2)}) collective-permute-start(bf16[128,640]{1,0:T(8,128)(2,1)S(1)} %add.140), channel_id=1, source_target_pairs={{0,112},{16,0},{32,16},{48,32},{64,48},{80,64},{96,80},{112,96},{1... | collective-permute-start | bytes 491528 | tf_op jit(solution)/shard_map/ppermute | solution.py:57
  139.6 3.6 %collective-permute-done.32 = bf16[128,1280]{1,0:T(8,128)(2,1)S(1)} collective-permute-done((bf16[128,1280]{1,0:T(8,128)(2,1)S(1)}, bf16[128,1280]{1,0:T(8,128)(2,1)S(1)}, u32[]{:S(2)}, u32[]{:S(2)}) %collective-permute-start.32) | collective-permute-done | bytes 327712 | tf_op jit(solution)/shard_map/ppermute | solution.py:57
  143.3 4.9 %collective-permute-done.34 = bf16[128,1280]{1,0:T(8,128)(2,1)S(1)} collective-permute-done((bf16[128,1280]{1,0:T(8,128)(2,1)S(1)}, bf16[128,1280]{1,0:T(8,128)(2,1)S(1)}, u32[]{:S(2)}, u32[]{:S(2)}) %collective-permute-start.34) | collective-permute-done | bytes 327712 | tf_op jit(solution)/shard_map/ppermute | solution.py:57
  150.2 9.1 %collective-permute-start.35 = (bf16[128,1920]{1,0:T(8,128)(2,1)S(1)}, bf16[128,1920]{1,0:T(8,128)(2,1)S(1)}, u32[]{:S(2)}, u32[]{:S(2)}) collective-permute-start(bf16[128,1920]{1,0:T(8,128)(2,1)S(1)} %pad_maximum_fusion), channel_id=1, source_target_pairs={{0,0},{1,128},{128,1},{129,129},{2,2},{3,130},{130,3},{131,131},{4... | collective-permute-start | bytes 1474568 | tf_op jit(solution)/shard_map/ppermute | solution.py:61
  163.3 2.5 %collective-permute-start.36 = (f32[2,128]{1,0:T(2,128)S(1)}, f32[2,128]{1,0:T(2,128)S(1)}, u32[]{:S(2)}, u32[]{:S(2)}) collective-permute-start(f32[2,128]{1,0:T(2,128)S(1)} %pad_maximum_fusion.10), channel_id=1, source_target_pairs={{0,0},{1,128},{2,2},{3,130},{128,1},{129,129},{130,3},{131,131},{4... | collective-permute-start | bytes 3080 | tf_op jit(solution)/shard_map/ppermute | solution.py:284
  165.9 2.3 %collective-permute-done.36 = f32[2,128]{1,0:T(2,128)S(1)} collective-permute-done((f32[2,128]{1,0:T(2,128)S(1)}, f32[2,128]{1,0:T(2,128)S(1)}, u32[]{:S(2)}, u32[]{:S(2)}) %collective-permute-start.36) | collective-permute-done | bytes 1056 | tf_op jit(solution)/shard_map/ppermute | solution.py:284
  (132 shorter events, 28.5 us)
Async XLA Ops:
  2.8 10.8 %collective-permute-start = (f32[2,128]{1,0:T(2,128)S(1)}, f32[2,128]{1,0:T(2,128)S(1)}, u32[]{:S(2)}, u32[]{:S(2)}) collective-permute-start(f32[2,128]{1,0:T(2,128)S(1)} %pad_maximum_fusion.9), channel_id=1, source_target_pairs={{0,1},{1,0},{2,3},{3,2},{4,5},{5,4},{6,7},{7,6},{8,9},{9,8},{10,11... | collective-permute-start | bytes 3080 | tf_op jit(solution)/shard_map/ppermute | solution.py:57
  18.8 8.7 %collective-permute-start.2 = (bf16[128,1280]{1,0:T(8,128)(2,1)S(1)}, bf16[128,1280]{1,0:T(8,128)(2,1)S(1)}, u32[]{:S(2)}, u32[]{:S(2)}) collective-permute-start(bf16[128,1280]{1,0:T(8,128)(2,1)S(1)} %pad_maximum_fusion.1), channel_id=1, source_target_pairs={{0,0},{1,128},{128,1},{129,129},{2,2},{3,130},{130,3},{131,131},{4... | collective-permute-start | bytes 983048 | tf_op jit(solution)/shard_map/ppermute | solution.py:61
  27.5 11.4 %collective-permute-start.3 = (bf16[128,1280]{1,0:T(8,128)(2,1)S(1)}, bf16[128,1280]{1,0:T(8,128)(2,1)S(1)}, u32[]{:S(2)}, u32[]{:S(2)}) collective-permute-start(bf16[128,1280]{1,0:T(8,128)(2,1)S(1)} %collective-permute-done.2.refs_0_), channel_id=1, source_target_pairs={{0,16},{16,32},{32,48},{48,64},{64,80},{80,96},{96,112},{112,0},{1... | collective-permute-start | bytes 983048 | tf_op jit(solution)/shard_map/ppermute | solution.py:57
  27.9 14.4 %collective-permute-start.7 = (bf16[128,1280]{1,0:T(8,128)(2,1)S(1)}, bf16[128,1280]{1,0:T(8,128)(2,1)S(1)}, u32[]{:S(2)}, u32[]{:S(2)}) collective-permute-start(bf16[128,1280]{1,0:T(8,128)(2,1)S(1)} %collective-permute-done.2.refs_0_), channel_id=1, source_target_pairs={{0,112},{16,0},{32,16},{48,32},{64,48},{80,64},{96,80},{112,96},{1... | collective-permute-start | bytes 983048 | tf_op jit(solution)/shard_map/ppermute | solution.py:57
  38.8 8.8 %collective-permute-start.4 = (bf16[128,1280]{1,0:T(8,128)(2,1)S(1)}, bf16[128,1280]{1,0:T(8,128)(2,1)S(1)}, u32[]{:S(2)}, u32[]{:S(2)}) collective-permute-start(bf16[128,1280]{1,0:T(8,128)(2,1)S(1)} %collective-permute-done.3.refs_1_), channel_id=1, source_target_pairs={{0,16},{16,32},{32,48},{48,64},{64,80},{80,96},{96,112},{112,0},{1... | collective-permute-start | bytes 983048 | tf_op jit(solution)/shard_map/ppermute | solution.py:57
  38.9 8.8 %collective-permute-start.11 = (bf16[128,1280]{1,0:T(8,128)(2,1)S(1)}, bf16[128,1280]{1,0:T(8,128)(2,1)S(1)}, u32[]{:S(2)}, u32[]{:S(2)}) collective-permute-start(bf16[128,1280]{1,0:T(8,128)(2,1)S(1)} %pad_maximum_fusion.2), channel_id=1, source_target_pairs={{0,0},{1,128},{128,1},{129,129},{2,2},{3,130},{130,3},{131,131},{4... | collective-permute-start | bytes 983048 | tf_op jit(solution)/shard_map/ppermute | solution.py:61
  42.2 9.2 %collective-permute-start.8 = (bf16[128,1280]{1,0:T(8,128)(2,1)S(1)}, bf16[128,1280]{1,0:T(8,128)(2,1)S(1)}, u32[]{:S(2)}, u32[]{:S(2)}) collective-permute-start(bf16[128,1280]{1,0:T(8,128)(2,1)S(1)} %collective-permute-done.7.refs_7_), channel_id=1, source_target_pairs={{0,112},{16,0},{32,16},{48,32},{64,48},{80,64},{96,80},{112,96},{1... | collective-permute-start | bytes 983048 | tf_op jit(solution)/shard_map/ppermute | solution.py:57
  47.6 7.8 %collective-permute-start.5 = (bf16[128,1280]{1,0:T(8,128)(2,1)S(1)}, bf16[128,1280]{1,0:T(8,128)(2,1)S(1)}, u32[]{:S(2)}, u32[]{:S(2)}) collective-permute-start(bf16[128,1280]{1,0:T(8,128)(2,1)S(1)} %collective-permute-done.4.refs_2_), channel_id=1, source_target_pairs={{0,16},{16,32},{32,48},{48,64},{64,80},{80,96},{96,112},{112,0},{1... | collective-permute-start | bytes 983048 | tf_op jit(solution)/shard_map/ppermute | solution.py:57
  47.6 10.6 %collective-permute-start.14 = (bf16[128,1280]{1,0:T(8,128)(2,1)S(1)}, bf16[128,1280]{1,0:T(8,128)(2,1)S(1)}, u32[]{:S(2)}, u32[]{:S(2)}) collective-permute-start(bf16[128,1280]{1,0:T(8,128)(2,1)S(1)} %collective-permute-done.11.refs_8_), channel_id=1, source_target_pairs={{0,12},{4,0},{8,4},{12,8},{1,13},{5,1},{9,5},{13,9},{2,14},{6,2},{... | collective-permute-start | bytes 983048 | tf_op jit(solution)/shard_map/ppermute | solution.py:57
  50.4 8.2 %collective-permute-start.13 = (bf16[128,1280]{1,0:T(8,128)(2,1)S(1)}, bf16[128,1280]{1,0:T(8,128)(2,1)S(1)}, u32[]{:S(2)}, u32[]{:S(2)}) collective-permute-start(bf16[128,1280]{1,0:T(8,128)(2,1)S(1)} %collective-permute-done.11.refs_8_), channel_id=1, source_target_pairs={{0,8},{4,12},{8,0},{12,4},{1,9},{5,13},{9,1},{13,5},{2,10},{6,14},... | collective-permute-start | bytes 983048 | tf_op jit(solution)/shard_map/ppermute | solution.py:57
  50.7 11.2 %collective-permute-start.12 = (bf16[128,1280]{1,0:T(8,128)(2,1)S(1)}, bf16[128,1280]{1,0:T(8,128)(2,1)S(1)}, u32[]{:S(2)}, u32[]{:S(2)}) collective-permute-start(bf16[128,1280]{1,0:T(8,128)(2,1)S(1)} %collective-permute-done.11.refs_8_), channel_id=1, source_target_pairs={{0,4},{4,8},{8,12},{12,0},{1,5},{5,9},{9,13},{13,1},{2,6},{6,10},{... | collective-permute-start | bytes 983048 | tf_op jit(solution)/shard_map/ppermute | solution.py:57
  51.4 10.5 %collective-permute-start.9 = (bf16[128,1280]{1,0:T(8,128)(2,1)S(1)}, bf16[128,1280]{1,0:T(8,128)(2,1)S(1)}, u32[]{:S(2)}, u32[]{:S(2)}) collective-permute-start(bf16[128,1280]{1,0:T(8,128)(2,1)S(1)} %collective-permute-done.8.refs_6_), channel_id=1, source_target_pairs={{0,112},{16,0},{32,16},{48,32},{64,48},{80,64},{96,80},{112,96},{1... | collective-permute-start | bytes 983048 | tf_op jit(solution)/shard_map/ppermute | solution.py:57
  55.4 7.0 %collective-permute-start.6 = (bf16[64,1280]{1,0:T(8,128)(2,1)S(1)}, bf16[64,1280]{1,0:T(8,128)(2,1)S(1)}, u32[]{:S(2)}, u32[]{:S(2)}) collective-permute-start(bf16[64,1280]{1,0:T(8,128)(2,1)S(1)} %slice.251), channel_id=1, source_target_pairs={{0,16},{16,32},{32,48},{48,64},{64,80},{80,96},{96,112},{112,0},{1... | collective-permute-start | bytes 491528 | tf_op jit(solution)/shard_map/ppermute | solution.py:57
  58.2 10.9 %collective-permute-start.15 = (bf16[128,1280]{1,0:T(8,128)(2,1)S(1)}, bf16[128,1280]{1,0:T(8,128)(2,1)S(1)}, u32[]{:S(2)}, u32[]{:S(2)}) collective-permute-start(bf16[128,1280]{1,0:T(8,128)(2,1)S(1)} %collective-permute-done.11.refs_8_), channel_id=1, source_target_pairs={{0,1},{1,0},{2,3},{3,2},{4,5},{5,4},{6,7},{7,6},{8,9},{9,8},{10,11... | collective-permute-start | bytes 983048 | tf_op jit(solution)/shard_map/ppermute | solution.py:57
  58.5 10.6 %collective-permute-start.18 = (bf16[128,1280]{1,0:T(8,128)(2,1)S(1)}, bf16[128,1280]{1,0:T(8,128)(2,1)S(1)}, u32[]{:S(2)}, u32[]{:S(2)}) collective-permute-start(bf16[128,1280]{1,0:T(8,128)(2,1)S(1)} %collective-permute-done.14.refs_11_), channel_id=1, source_target_pairs={{0,1},{1,0},{2,3},{3,2},{4,5},{5,4},{6,7},{7,6},{8,9},{9,8},{10,11... | collective-permute-start | bytes 983048 | tf_op jit(solution)/shard_map/ppermute | solution.py:57
  61.9 7.2 %collective-permute-start.17 = (bf16[128,1280]{1,0:T(8,128)(2,1)S(1)}, bf16[128,1280]{1,0:T(8,128)(2,1)S(1)}, u32[]{:S(2)}, u32[]{:S(2)}) collective-permute-start(bf16[128,1280]{1,0:T(8,128)(2,1)S(1)} %collective-permute-done.13.refs_10_), channel_id=1, source_target_pairs={{0,1},{1,0},{2,3},{3,2},{4,5},{5,4},{6,7},{7,6},{8,9},{9,8},{10,11... | collective-permute-start | bytes 983048 | tf_op jit(solution)/shard_map/ppermute | solution.py:57
  61.9 7.3 %collective-permute-start.16 = (bf16[128,1280]{1,0:T(8,128)(2,1)S(1)}, bf16[128,1280]{1,0:T(8,128)(2,1)S(1)}, u32[]{:S(2)}, u32[]{:S(2)}) collective-permute-start(bf16[128,1280]{1,0:T(8,128)(2,1)S(1)} %collective-permute-done.12.refs_9_), channel_id=1, source_target_pairs={{0,1},{1,0},{2,3},{3,2},{4,5},{5,4},{6,7},{7,6},{8,9},{9,8},{10,11... | collective-permute-start | bytes 983048 | tf_op jit(solution)/shard_map/ppermute | solution.py:57
  62.5 6.7 %collective-permute-start.10 = (bf16[64,1280]{1,0:T(8,128)(2,1)S(1)}, bf16[64,1280]{1,0:T(8,128)(2,1)S(1)}, u32[]{:S(2)}, u32[]{:S(2)}) collective-permute-start(bf16[64,1280]{1,0:T(8,128)(2,1)S(1)} %slice.252), channel_id=1, source_target_pairs={{0,112},{16,0},{32,16},{48,32},{64,48},{80,64},{96,80},{112,96},{1... | collective-permute-start | bytes 491528 | tf_op jit(solution)/shard_map/ppermute | solution.py:57
  78.8 5.9 %collective-permute-start.19 = (f32[24,1024]{1,0:T(8,128)S(1)}, f32[24,1024]{1,0:T(8,128)S(1)}, u32[]{:S(2)}, u32[]{:S(2)}) collective-permute-start(f32[24,1024]{1,0:T(8,128)S(1)} %block_stats.1), channel_id=1, source_target_pairs={{0,16},{16,32},{32,48},{48,64},{64,80},{80,96},{96,112},{112,0},{1... | collective-permute-start | bytes 294920 | tf_op jit(solution)/shard_map/ppermute | solution.py:57
  84.8 13.6 %collective-permute-start.22 = (f32[24,1024]{1,0:T(8,128)S(1)}, f32[24,1024]{1,0:T(8,128)S(1)}, u32[]{:S(2)}, u32[]{:S(2)}) collective-permute-start(f32[24,1024]{1,0:T(8,128)S(1)} %pad_maximum_fusion.3), channel_id=1, source_target_pairs={{0,64},{16,80},{32,96},{48,112},{64,0},{80,16},{96,32},{112,48},{1... | collective-permute-start | bytes 294920 | tf_op jit(solution)/shard_map/ppermute | solution.py:57
  88.9 9.4 %collective-permute-start.21 = (f32[24,1024]{1,0:T(8,128)S(1)}, f32[24,1024]{1,0:T(8,128)S(1)}, u32[]{:S(2)}, u32[]{:S(2)}) collective-permute-start(f32[24,1024]{1,0:T(8,128)S(1)} %pad_maximum_fusion.3), channel_id=1, source_target_pairs={{0,96},{16,112},{32,0},{48,16},{64,32},{80,48},{96,64},{112,80},{1... | collective-permute-start | bytes 294920 | tf_op jit(solution)/shard_map/ppermute | solution.py:57
  89.3 9.0 %collective-permute-start.20 = (f32[24,1024]{1,0:T(8,128)S(1)}, f32[24,1024]{1,0:T(8,128)S(1)}, u32[]{:S(2)}, u32[]{:S(2)}) collective-permute-start(f32[24,1024]{1,0:T(8,128)S(1)} %pad_maximum_fusion.3), channel_id=1, source_target_pairs={{0,32},{16,48},{32,64},{48,80},{64,96},{80,112},{96,0},{112,16},{1... | collective-permute-start | bytes 294920 | tf_op jit(solution)/shard_map/ppermute | solution.py:57
  115.8 21.0 %collective-permute-start.31 = (bf16[512,1280]{1,0:T(8,128)(2,1)}, bf16[512,1280]{1,0:T(8,128)(2,1)S(1)}, u32[]{:S(2)}, u32[]{:S(2)}) collective-permute-start(bf16[512,1280]{1,0:T(8,128)(2,1)} %get-tuple-element.22), channel_id=1, source_target_pairs={{0,1},{1,0},{2,3},{3,2},{4,5},{5,4},{6,7},{7,6},{8,9},{9,8},{10,11... | collective-permute-start | bytes 3932168 | tf_op jit(solution)/shard_map/ppermute | solution.py:57
  122.2 6.2 %collective-permute-start.28 = (bf16[128,640]{1,0:T(8,128)(2,1)S(1)}, bf16[128,640]{1,0:T(8,128)(2,1)S(1)}, u32[]{:S(2)}, u32[]{:S(2)}) collective-permute-start(bf16[128,640]{1,0:T(8,128)(2,1)S(1)} %pad_add_fusion), channel_id=1, source_target_pairs={{0,16},{16,32},{32,48},{48,64},{64,80},{80,96},{96,112},{112,0},{1... | collective-permute-start | bytes 491528 | tf_op jit(solution)/shard_map/ppermute | solution.py:57
  128.5 5.5 %collective-permute-start.29 = (bf16[128,640]{1,0:T(8,128)(2,1)S(1)}, bf16[128,640]{1,0:T(8,128)(2,1)S(1)}, u32[]{:S(2)}, u32[]{:S(2)}) collective-permute-start(bf16[128,640]{1,0:T(8,128)(2,1)S(1)} %add.143), channel_id=1, source_target_pairs={{0,16},{16,32},{32,48},{48,64},{64,80},{80,96},{96,112},{112,0},{1... | collective-permute-start | bytes 491528 | tf_op jit(solution)/shard_map/ppermute | solution.py:57
  134.0 5.5 %collective-permute-start.30 = (bf16[128,640]{1,0:T(8,128)(2,1)S(1)}, bf16[128,640]{1,0:T(8,128)(2,1)S(1)}, u32[]{:S(2)}, u32[]{:S(2)}) collective-permute-start(bf16[128,640]{1,0:T(8,128)(2,1)S(1)} %add.144), channel_id=1, source_target_pairs={{0,16},{16,32},{32,48},{48,64},{64,80},{80,96},{96,112},{112,0},{1... | collective-permute-start | bytes 491528 | tf_op jit(solution)/shard_map/ppermute | solution.py:57
  137.2 6.0 %collective-permute-start.32 = (bf16[128,1280]{1,0:T(8,128)(2,1)S(1)}, bf16[128,1280]{1,0:T(8,128)(2,1)S(1)}, u32[]{:S(2)}, u32[]{:S(2)}) collective-permute-start(bf16[128,1280]{1,0:T(8,128)(2,1)S(1)} %get-tuple-element.29), channel_id=1, source_target_pairs={{0,12},{4,0},{8,4},{12,8},{1,13},{5,1},{9,5},{13,9},{2,14},{6,2},{... | collective-permute-start | bytes 983048 | tf_op jit(solution)/shard_map/ppermute | solution.py:57
  137.7 10.5 %collective-permute-start.34 = (bf16[128,1280]{1,0:T(8,128)(2,1)S(1)}, bf16[128,1280]{1,0:T(8,128)(2,1)S(1)}, u32[]{:S(2)}, u32[]{:S(2)}) collective-permute-start(bf16[128,1280]{1,0:T(8,128)(2,1)S(1)} %get-tuple-element.30), channel_id=1, source_target_pairs={{0,4},{4,8},{8,12},{12,0},{1,5},{5,9},{9,13},{13,1},{2,6},{6,10},{... | collective-permute-start | bytes 983048 | tf_op jit(solution)/shard_map/ppermute | solution.py:57
  138.8 11.2 %collective-permute-start.33 = (bf16[128,1280]{1,0:T(8,128)(2,1)S(1)}, bf16[128,1280]{1,0:T(8,128)(2,1)S(1)}, u32[]{:S(2)}, u32[]{:S(2)}) collective-permute-start(bf16[128,1280]{1,0:T(8,128)(2,1)S(1)} %get-tuple-element.31), channel_id=1, source_target_pairs={{0,8},{4,12},{8,0},{12,4},{1,9},{5,13},{9,1},{13,5},{2,10},{6,14},... | collective-permute-start | bytes 983048 | tf_op jit(solution)/shard_map/ppermute | solution.py:57
  150.2 18.0 %collective-permute-start.35 = (bf16[128,1920]{1,0:T(8,128)(2,1)S(1)}, bf16[128,1920]{1,0:T(8,128)(2,1)S(1)}, u32[]{:S(2)}, u32[]{:S(2)}) collective-permute-start(bf16[128,1920]{1,0:T(8,128)(2,1)S(1)} %pad_maximum_fusion), channel_id=1, source_target_pairs={{0,0},{1,128},{128,1},{129,129},{2,2},{3,130},{130,3},{131,131},{4... | collective-permute-start | bytes 1474568 | tf_op jit(solution)/shard_map/ppermute | solution.py:61
  159.4 6.5 %collective-permute-start.39 = (f32[2,128]{1,0:T(2,128)S(1)}, f32[2,128]{1,0:T(2,128)S(1)}, u32[]{:S(2)}, u32[]{:S(2)}) collective-permute-start(f32[2,128]{1,0:T(2,128)S(1)} %pad_maximum_fusion.10), channel_id=1, source_target_pairs={{0,3},{1,131},{2,1},{3,129},{128,2},{129,130},{130,0},{131,128},{4... | collective-permute-start | bytes 3080 | tf_op jit(solution)/shard_map/ppermute | solution.py:284
  159.5 6.4 %collective-permute-start.38 = (f32[2,128]{1,0:T(2,128)S(1)}, f32[2,128]{1,0:T(2,128)S(1)}, u32[]{:S(2)}, u32[]{:S(2)}) collective-permute-start(f32[2,128]{1,0:T(2,128)S(1)} %pad_maximum_fusion.10), channel_id=1, source_target_pairs={{0,1},{1,129},{2,3},{3,131},{128,0},{129,128},{130,2},{131,130},{4... | collective-permute-start | bytes 3080 | tf_op jit(solution)/shard_map/ppermute | solution.py:284
  (17 other events, 120.6 us)
